TPU v7x, 512 devices: a whole 4x8x8 slice. The times are simulated.
512 devices in a mesh: lat: 16 (over y_hi, z), lon: 32 (over x, y_lo, core).
Axes of the slice: x: 4, y: 8 (y_hi: 2, y_lo: 4; y = y_hi * 4 + y_lo), z: 8, core: 2. Of those that a mesh axis runs over, the one named last changes fastest.
Arguments:
- fields: bfloat16 [128, 1024, 256], P('lat', 'lon'), may hold values from -6 to 6
- kernel: bfloat16 [3, 3, 256, 256], replicated, may hold values from -0.125 to 0.125
- bias: float32 [256], replicated, may hold values from -3 to 3
- target: bfloat16 [128, 1024, 256], P('lat', 'lon'), may hold values from -12 to 12
- tile_list: int32 [1024], replicated, may hold values from 0 to 1023, each once
- tail_count: int32 [32], replicated, may hold values from 384 to 768
- region_weight: float32 [32], replicated, may hold values from 2000 to 20000
Outputs:
- grad_fields: bfloat16 [128, 1024, 256], P('lat', 'lon')
- grad_kernel: bfloat16 [3, 3, 256, 256], replicated
- grad_bias: float32 [256], replicated
- region_loss: float32 [32], replicated
Inputs may be any that keep to these rules, and one draw needn't show every extreme that they name: `tile_list`: each tile number appears once, so the regions split the grid into 32 parts of 32 tiles each.
All inputs are finite; a program needn't handle non-finite values.
Results may differ from a plain program's by a relative error of at most 0.0049.
Values may be sent and summed in bfloat16 or wider, within the bound.
A program may use at most 64 MiB of HBM per device.

v0:
```python
import jax
import jax.numpy as jnp
from jax import lax
from jax.sharding import PartitionSpec as P

NREG = 32
ITERS = 6


SMOOTH = 0.05
STEP_LIMIT = 0.3
DAMPING = 0.4
GELU_SCALE = 0.7978845608
GELU_CUBIC = 0.044715


def with_halo(cells, sides, width, closed):
    for axis, dim in sides:
        count = lax.axis_size(axis)
        ends = count if closed else count - 1
        head = lax.slice_in_dim(cells, 0, width, axis=dim)
        tail = lax.slice_in_dim(cells, cells.shape[dim] - width, cells.shape[dim], axis=dim)
        cells = jnp.concatenate(
            [
                lax.ppermute(tail, axis, [(i, (i + 1) % count) for i in range(ends)]),
                cells,
                lax.ppermute(head, axis, [((i + 1) % count, i) for i in range(ends)]),
            ],
            axis=dim,
        )
    return cells


def gelu_pair(value):
    inner = GELU_SCALE * (value + GELU_CUBIC * value * value * value)
    tangent = jnp.tanh(inner)
    act = 0.5 * value * (1.0 + tangent)
    slope = 0.5 * (1.0 + tangent) + 0.5 * value * (1.0 - tangent * tangent) * GELU_SCALE * (
        1.0 + 3.0 * GELU_CUBIC * value * value
    )
    return (act, slope)


def extend(field):
    wrapped = with_halo(field, (("lon", 1),), 1, True)
    return with_halo(wrapped, (("lat", 0),), 1, False)


def on_device(fields, kernel, bias, target, tile_list, tail_count, region_weight):
    rows, cols, chans = fields.shape
    count_pts = rows * cols
    padded = extend(fields)
    pre = jnp.zeros((count_pts, chans), jnp.float32)
    for a in range(3):
        for b in range(3):
            patch = padded[a : a + rows, b : b + cols].reshape(count_pts, chans)
            pre = pre + jnp.dot(patch, kernel[a, b], preferred_element_type=jnp.float32)
    pre = pre + bias
    act, slope = gelu_pair(pre)
    diff = act - target.reshape(count_pts, chans).astype(jnp.float32)
    nlat = rows * lax.axis_size("lat")
    row_ids = (lax.axis_index("lat") * rows + jnp.arange(rows)).astype(jnp.float32)
    lat_w = jnp.cos(jnp.pi * (row_ids + 0.5) / nlat - jnp.pi / 2)
    err = lat_w[:, None] * jnp.mean(diff * diff, axis=1).reshape(rows, cols)
    tile_rows = rows // 8
    tile_cols = cols // 16
    across = cols * lax.axis_size("lon") // 16
    row_tiles = lax.axis_index("lat") * tile_rows + jnp.arange(tile_rows)
    col_tiles = lax.axis_index("lon") * tile_cols + jnp.arange(tile_cols)
    tile_ids = (row_tiles[:, None] * across + col_tiles[None, :]).reshape(-1)
    lists = tile_list.reshape(NREG, -1)
    member = jnp.sum((lists[:, :, None] == tile_ids[None, None, :]).astype(jnp.float32), axis=1)
    count = tail_count.astype(jnp.float32)
    region_points = float(lists.shape[1] * 128)

    def per_tile(values):
        tiles = values.reshape(tile_rows, 8, tile_cols, 16).sum(axis=(1, 3)).reshape(-1)
        return jnp.dot(member, tiles, precision=lax.Precision.HIGHEST)

    def to_points(region_values):
        tiles = jnp.dot(region_values, member, precision=lax.Precision.HIGHEST).reshape(
            tile_rows, 1, tile_cols, 1
        )
        return jnp.broadcast_to(tiles, (tile_rows, 8, tile_cols, 16)).reshape(rows, cols)

    err_total = lax.psum(per_tile(err), ("lat", "lon"))
    thresh = 2.0 * err_total / region_points
    for step in range(ITERS):
        sig = jax.nn.sigmoid((err - to_points(thresh)) / SMOOTH)
        above, spread = lax.psum((per_tile(sig), per_tile(sig * (1.0 - sig))), ("lat", "lon"))
        thresh = thresh + jnp.clip(
            DAMPING * SMOOTH * (above - count) / (spread + 1.0), -STEP_LIMIT, STEP_LIMIT
        )
    scaled = (err - to_points(thresh)) / SMOOTH
    sig = jax.nn.sigmoid(scaled)
    soft_part = per_tile(SMOOTH * jax.nn.softplus(scaled))
    d_err = to_points(region_weight / count) * sig * lat_w[:, None]
    grad_pre = (d_err.reshape(count_pts, 1) * (2.0 / chans) * diff * slope).astype(jnp.bfloat16)
    gpad = extend(grad_pre.reshape(rows, cols, chans))
    grad_fields = jnp.zeros((count_pts, chans), jnp.float32)
    taps_out = []
    for a in range(3):
        taps_row = []
        for b in range(3):
            patch = gpad[2 - a : 2 - a + rows, 2 - b : 2 - b + cols].reshape(count_pts, chans)
            grad_fields = grad_fields + lax.dot_general(
                patch, kernel[a, b], (((1,), (1,)), ((), ())), preferred_element_type=jnp.float32
            )
            source = padded[a : a + rows, b : b + cols].reshape(count_pts, chans)
            taps_row.append(
                lax.dot_general(
                    source, grad_pre, (((0,), (0,)), ((), ())), preferred_element_type=jnp.float32
                )
            )
        taps_out.append(jnp.stack(taps_row))
    local_kernel = jnp.stack(taps_out)
    local_bias = jnp.sum(grad_pre.astype(jnp.float32), axis=0)
    total_kernel, grad_bias, soft_total = lax.psum(
        (local_kernel, local_bias, soft_part), ("lat", "lon")
    )
    grad_kernel = total_kernel.astype(jnp.bfloat16)
    region_loss = thresh + soft_total / count
    return (
        grad_fields.reshape(rows, cols, chans).astype(jnp.bfloat16),
        grad_kernel,
        grad_bias,
        region_loss,
    )


def solution(mesh):
    placed = (P("lat", "lon", None), P(), P(), P("lat", "lon", None), P(), P(), P())
    return jax.shard_map(
        on_device,
        mesh=mesh,
        in_specs=placed,
        out_specs=(P("lat", "lon", None), P(), P(), P()),
        check_vma=False,
    )
```

profile of v0, /device:TPU:1, one launch (start us, length us, event | category | flops | bytes accessed | tf_op | source)
XLA Modules:
  0.0 832.5 jit_solution(16918991335474666280)
XLA Ops:
  0.6 0.8 fusion.104
  1.5 4.6 collective-permute-start
  6.1 6.1 collective-permute-start.1
  12.2 0.8 eq.15
  13.0 1.1 fusion.25
  14.4 0.8 pad_maximum_fusion.12
  15.1 1.3 collective-permute-start.2
  16.5 1.4 collective-permute-start.3
  17.9 1.1 pad_maximum_fusion.5
  19.0 2.4 collective-permute-done.3
  23.1 0.5 copy-done.3
  23.6 0.4 multiply_reduce_fusion
  24.3 109.0 %psum.112 = f32[32]{0:T(128)S(1)} all-reduce(f32[32]{0:T(128)S(1)} %convolution_bitcast_fusion.29), channel_id=1, replica_groups=mesh['lat'=16,'lon'=32] {'lat','lon'}, use_global_device_ids=true, to_apply=%region_3.0 | all-reduce | flops 32 | bytes 256 | tf_op jit(solution)/shard_map/psum | solution.py:86
  133.9 94.5 %all-reduce.6 = (f32[32]{0:T(128)S(1)}, f32[32]{0:T(128)S(1)}) all-reduce(f32[32]{0:T(128)S(1)} %convolution_bitcast_fusion.26, f32[32]{0:T(128)S(1)} %convolution_bitcast_fusion.27), channel_id=1, replica_groups=mesh['lat'=16,'lon'=32] {'lat','lon'}, use_global_device_ids=true, to_apply=%region_7.0 | all-reduce | flops 64 | bytes 512 | tf_op jit(solution)/shard_map/psum | solution.py:90
  229.1 94.3 %all-reduce.5 = (f32[32]{0:T(128)S(1)}, f32[32]{0:T(128)S(1)}) all-reduce(f32[32]{0:T(128)S(1)} %convolution_bitcast_fusion.23, f32[32]{0:T(128)S(1)} %convolution_bitcast_fusion.24), channel_id=1, replica_groups=mesh['lat'=16,'lon'=32] {'lat','lon'}, use_global_device_ids=true, to_apply=%region_11.12 | all-reduce | flops 64 | bytes 512 | tf_op jit(solution)/shard_map/psum | solution.py:90
  323.9 94.4 %all-reduce.4 = (f32[32]{0:T(128)S(1)}, f32[32]{0:T(128)S(1)}) all-reduce(f32[32]{0:T(128)S(1)} %convolution_bitcast_fusion.20, f32[32]{0:T(128)S(1)} %convolution_bitcast_fusion.21), channel_id=1, replica_groups=mesh['lat'=16,'lon'=32] {'lat','lon'}, use_global_device_ids=true, to_apply=%region_15.16 | all-reduce | flops 64 | bytes 512 | tf_op jit(solution)/shard_map/psum | solution.py:90
  419.0 95.3 %all-reduce.3 = (f32[32]{0:T(128)S(1)}, f32[32]{0:T(128)S(1)}) all-reduce(f32[32]{0:T(128)S(1)} %convolution_bitcast_fusion.17, f32[32]{0:T(128)S(1)} %convolution_bitcast_fusion.18), channel_id=1, replica_groups=mesh['lat'=16,'lon'=32] {'lat','lon'}, use_global_device_ids=true, to_apply=%region_19.20 | all-reduce | flops 64 | bytes 512 | tf_op jit(solution)/shard_map/psum | solution.py:90
  515.0 94.4 %all-reduce.2 = (f32[32]{0:T(128)S(1)}, f32[32]{0:T(128)S(1)}) all-reduce(f32[32]{0:T(128)S(1)} %convolution_bitcast_fusion.14, f32[32]{0:T(128)S(1)} %convolution_bitcast_fusion.15), channel_id=1, replica_groups=mesh['lat'=16,'lon'=32] {'lat','lon'}, use_global_device_ids=true, to_apply=%region_23.24 | all-reduce | flops 64 | bytes 512 | tf_op jit(solution)/shard_map/psum | solution.py:90
  610.1 95.2 %all-reduce.1 = (f32[32]{0:T(128)S(1)}, f32[32]{0:T(128)S(1)}) all-reduce(f32[32]{0:T(128)S(1)} %convolution_bitcast_fusion.11, f32[32]{0:T(128)S(1)} %convolution_bitcast_fusion.12), channel_id=1, replica_groups=mesh['lat'=16,'lon'=32] {'lat','lon'}, use_global_device_ids=true, to_apply=%region_27.28 | all-reduce | flops 64 | bytes 512 | tf_op jit(solution)/shard_map/psum | solution.py:90
  705.7 0.2 convert_reduce_fusion
  707.1 0.2 convolution_bitcast_fusion.4
  708.2 0.2 fusion.23
  708.9 4.1 collective-permute-start.4
  713.0 1.9 collective-permute-start.5
  714.9 108.1 %all-reduce.8 = (bf16[3,3,256,256]{3,2,1,0:T(8,128)(2,1)}, f32[256]{0:T(256)}, f32[32]{0:T(128)S(1)}) all-reduce(f32[3,3,256,256]{3,2,1,0:T(8,128)S(1)} %pad_maximum_fusion, f32[256]{0:T(256)S(1)} %get-tuple-element.31, f32[32]{0:T(128)S(1)} %convolution_bitcast_fusion.9), channel_id=1, replica_groups=mesh['lat'=16,'lon'=32] {'lat','lon'}, use_global_device_ids=true, to_apply=%region_28.29 | all-reduce | flops 590112 | bytes 3541248 | tf_op jit(solution)/shard_map/psum | solution.py:118
  823.1 0.5 divide_add_fusion
  823.6 1.3 collective-permute-start.6
  824.9 4.0 collective-permute-start.7
  829.0 0.8 collective-permute-done.7
  830.5 0.2 convolution_add_fusion.5
  831.2 0.2 fusion
  831.6 0.9 fusion.5
  (98 shorter events, 10.3 us)
Async XLA Ops:
  0.6 20.8 %copy-start.2 = (bf16[8,32,256]{2,1,0:T(8,128)(2,1)S(1)}, bf16[8,32,256]{2,1,0:T(8,128)(2,1)}, u32[]{:S(2)}) copy-start(bf16[8,32,256]{2,1,0:T(8,128)(2,1)} %param.7) | copy-start | bytes 393220
  1.5 12.9 %collective-permute-start = (bf16[8,1,256]{2,1,0:T(2,128)(2,1)S(1)}, bf16[8,1,256]{2,1,0:T(2,128)(2,1)S(1)}, u32[]{:S(2)}, u32[]{:S(2)}) collective-permute-start(bf16[8,1,256]{2,1,0:T(2,128)(2,1)S(1)} %get-tuple-element.59), channel_id=1, source_target_pairs={{0,1},{1,2},{2,3},{3,4},{4,5},{5,6},{6,7},{7,8},{8,9},{9,10},{10,1... | collective-permute-start | bytes 12296 | tf_op jit(solution)/shard_map/ppermute | solution.py:25
  6.1 8.3 collective-permute-start.1
  15.1 3.8 collective-permute-start.2
  16.4 5.2 copy-start
  16.5 5.0 collective-permute-start.3
  22.7 0.9 copy-start.3
  22.7 0.9 copy-start.5
  22.9 205.6 %copy-start.4 = (s32[32]{0:T(128)S(1)}, s32[32]{0:T(128)}, u32[]{:S(2)}) copy-start(s32[32]{0:T(128)} %param.12) | copy-start | bytes 388
  22.9 396.0 %copy-start.6 = (f32[32]{0:T(128)S(1)}, f32[32]{0:T(128)}, u32[]{:S(2)}) copy-start(f32[32]{0:T(128)} %param.13) | copy-start | bytes 388
  708.9 114.7 %collective-permute-start.4 = (bf16[8,1,256]{2,1,0:T(2,128)(2,1)S(1)}, bf16[8,1,256]{2,1,0:T(2,128)(2,1)S(1)}, u32[]{:S(2)}, u32[]{:S(2)}) collective-permute-start(bf16[8,1,256]{2,1,0:T(2,128)(2,1)S(1)} %get-tuple-element.55), channel_id=1, source_target_pairs={{0,1},{1,2},{2,3},{3,4},{4,5},{5,6},{6,7},{7,8},{8,9},{9,10},{10,1... | collective-permute-start | bytes 12296 | tf_op jit(solution)/shard_map/ppermute | solution.py:25
  713.0 110.6 %collective-permute-start.5 = (bf16[8,1,256]{2,1,0:T(2,128)(2,1)S(1)}, bf16[8,1,256]{2,1,0:T(2,128)(2,1)S(1)}, u32[]{:S(2)}, u32[]{:S(2)}) collective-permute-start(bf16[8,1,256]{2,1,0:T(2,128)(2,1)S(1)} %get-tuple-element.56), channel_id=1, source_target_pairs={{1,0},{2,1},{3,2},{4,3},{5,4},{6,5},{7,6},{8,7},{9,8},{10,9},{11,1... | collective-permute-start | bytes 12296 | tf_op jit(solution)/shard_map/ppermute | solution.py:27
  823.1 6.9 copy-start.1
  823.6 5.4 collective-permute-start.6
  824.9 4.9 collective-permute-start.7
where the time goes:
time: 843 us; the launch traced here: 833 us
  blocking collectives  785 us (93%)
  starting transfers between devices  24.7 us (3%)
  matrix products  10.3 us (1%)
    psum x6, blocking collectives, on_device(): lax.psum((per_tile(sig), per_tile(sig * (1.0 - sig))), ('lat', 'lon'))  568 us
    psum x1, blocking collectives, on_device(): err_total = lax.psum(per_tile(err), ('lat', 'lon'))  109 us
    psum x1, blocking collectives, on_device(): lax.psum((local_kernel, local_bias, soft_part), ('lat', 'lon'))  108 us
  transfers between devices with their start and end apart: 8, of which 2 were waited for; matrix products, arithmetic and copies ran while one was open for 0% of the time, Pallas kernels for 0%

commit v1 on v0

v1 whole, which is shorter than its diff:
```python
import functools

import jax
import jax.numpy as jnp
import numpy as np
from jax import lax
from jax.experimental import pallas as pl
from jax.experimental.pallas import tpu as pltpu
from jax.sharding import PartitionSpec as P

NREG = 32
ITERS = 6
SMOOTH = 0.05
STEP_LIMIT = 0.3
DAMPING = 0.4
GELU_SCALE = 0.7978845608
GELU_CUBIC = 0.044715

MESH = pl.DeviceIdType.MESH
NLAT, NLON = 16, 32
NX, NY, NZ = 4, 8, 8
ROWS, COLS, C = 8, 32, 256
NPTS = ROWS * COLS
F32, BF16 = jnp.float32, jnp.bfloat16


def gelu_pair(value):
    inner = GELU_SCALE * (value + GELU_CUBIC * value * value * value)
    tangent = jnp.tanh(inner)
    act = 0.5 * value * (1.0 + tangent)
    slope = 0.5 * (1.0 + tangent) + 0.5 * value * (1.0 - tangent * tangent) * GELU_SCALE * (
        1.0 + 3.0 * GELU_CUBIC * value * value
    )
    return act, slope


def position():
    lat, lon = lax.axis_index("lat"), lax.axis_index("lon")
    x, y, z, core = lon // 8, (lat // 8) * 4 + (lon % 8) // 2, lat % 8, lon % 2
    return lat, lon, x, y, z, core


def device_at(x, y, z, core):
    return ((y // 4) * 8 + z, x * 8 + (y % 4) * 2 + core)


def halo_peers(lat, lon):
    steps = ((0, -1), (0, 1), (-1, 0), (1, 0), (-1, -1), (-1, 1), (1, -1), (1, 1))
    return [((lat + dl + NLAT) % NLAT, (lon + dn + NLON) % NLON) for dl, dn in steps]


def line_peers(x, y, z, core):
    zs = [device_at(x, y, (z + k) % NZ, core) for k in range(1, NZ)]
    ys = [device_at(x, (y + k) % NY, z, core) for k in range(1, NY)]
    xs = [device_at((x + k) % NX, y, z, core) for k in range(1, NX)]
    return zs, ys, xs, [device_at(x, y, z, 1 - core)]


def body(fields, w, bias, target, small, lw,
         gf_out, gk_out, gb_out, rl_out,
         pad, shifted, colbuf, rowbuf, colrec, rowrec, ds_ref, r1, r4, pt, es,
         hsend, hrecv, gsend, grecv, zsend, zrecv):
    lat, lon, x, y, z, core = position()
    zs, ys, xs, cs = line_peers(x, y, z, core)
    halos = halo_peers(lat, lon)

    barrier = pltpu.get_barrier_semaphore()
    everyone = halos + zs + ys + xs + cs
    for peer in everyone:
        pl.semaphore_signal(barrier, inc=1, device_id=peer, device_id_type=MESH)

    def remote(src, dst, send, recv, peer):
        return pltpu.make_async_remote_copy(
            src_ref=src, dst_ref=dst, send_sem=send, recv_sem=recv,
            device_id=peer, device_id_type=MESH,
        )

    def pack(n):
        for i in range(ROWS):
            colbuf[n, 0, i : i + 1, :] = pad[1 + i, 8:9, :]
            colbuf[n, 1, i : i + 1, :] = pad[1 + i, 7 + COLS : 8 + COLS, :]

    def halo_copies(n):
        west, east = colbuf.at[n, 0], colbuf.at[n, 1]
        north, south = rowbuf.at[n, 0], rowbuf.at[n, 1]
        sources = (west, east, north, south, west, east, west, east)
        targets = (
            colrec.at[n, 0], colrec.at[n, 1], rowrec.at[n, 0], rowrec.at[n, 1],
            colrec.at[n, 2], colrec.at[n, 3], colrec.at[n, 4], colrec.at[n, 5],
        )
        return [
            remote(sources[d], targets[d], hsend.at[n, d], hrecv.at[n, d], halos[d])
            for d in range(8)
        ]

    below = (lat < NLAT - 1).astype(F32)
    above_me = (lat > 0).astype(F32)

    def place(n):
        for i in range(ROWS):
            pad[1 + i, 8 + COLS : 9 + COLS, :] = colrec[n, 0, i : i + 1, :]
            pad[1 + i, 7:8, :] = colrec[n, 1, i : i + 1, :]
        last, end = ROWS + 1, 8 + COLS
        pad[last, 8:end, :] = rowrec[n, 0].astype(F32) * below
        pad[0, 8:end, :] = rowrec[n, 1].astype(F32) * above_me
        pad[last, end : end + 1, :] = colrec[n, 2, 0:1, :] * below
        pad[last, 7:8, :] = colrec[n, 3, 0:1, :] * below
        pad[0, end : end + 1, :] = colrec[n, 4, ROWS - 1 : ROWS, :] * above_me
        pad[0, 7:8, :] = colrec[n, 5, ROWS - 1 : ROWS, :] * above_me
        for b in range(3):
            for t in range(2):
                at = 7 + b + 16 * t
                shifted[b, t] = pad[:, at : at + 16, :].astype(BF16)

    def patch(a, b):
        parts = [shifted[b, t, a : a + ROWS].reshape(NPTS // 2, C) for t in range(2)]
        return jnp.concatenate(parts, axis=0)

    for r in range(ROWS):
        pad[1 + r, 8 : 8 + COLS, :] = fields[r].astype(F32)
    pack(0)
    rowbuf[0, 0] = fields[0]
    rowbuf[0, 1] = fields[ROWS - 1]
    pl.semaphore_wait(barrier, len(everyone))
    halo = halo_copies(0)
    for copy in halo:
        copy.start()

    slot = lax.broadcasted_iota(jnp.int32, (1024, 128), 0)
    st, sz, sy = slot & 1, (slot >> 1) & 7, (slot >> 4) & 7
    sx, sc = (slot >> 7) & 3, slot >> 9
    tile = ((sy >> 2) * 8 + sz) * 64 + (sx * 8 + (sy & 3) * 2 + sc) * 2 + st
    tile = tile.astype(F32)
    for blk in range(8):
        pt[:, 128 * blk : 128 * (blk + 1)] = jnp.where(
            tile == small[blk : blk + 1, :], 1.0, 0.0
        ).astype(BF16)

    for copy in halo:
        copy.wait()
    place(0)

    pre = jnp.zeros((NPTS, C), F32)
    for a in range(3):
        for b in range(3):
            k = 3 * a + b
            pre = pre + jnp.dot(
                patch(a, b), w[k * C : (k + 1) * C, :], preferred_element_type=F32
            )
    pre = pre + bias[...]
    act, slope = gelu_pair(pre)
    aim = jnp.concatenate(
        [target[:, 16 * t : 16 * (t + 1), :].reshape(NPTS // 2, C) for t in range(2)], axis=0
    )
    diff = act - aim.astype(F32)
    ds_ref[...] = diff * slope
    square = diff * diff
    prow = (lax.broadcasted_iota(jnp.int32, (1, NPTS), 1) >> 4) & 7
    pcol = (lax.broadcasted_iota(jnp.int32, (NPTS, 1), 0) >> 4) & 7
    lw_row, lw_col = jnp.zeros((1, NPTS), F32), jnp.zeros((NPTS, 1), F32)
    for i in range(ROWS):
        weight = lw[lat * ROWS + i]
        lw_row = jnp.where(prow == i, weight, lw_row)
        lw_col = jnp.where(pcol == i, weight, lw_col)
    err_row = lax.dot_general(
        jnp.ones((8, C), F32), square, (((1,), (1,)), ((), ())),
        precision=lax.Precision.HIGHEST, preferred_element_type=F32,
    )[0:1, :] * (1.0 / C) * lw_row
    r1[z, 0:1, :] = err_row[:, :128]
    r1[z, 1:2, :] = err_row[:, 128:]

    def exchange(ref, slot_id, peers, first):
        copies = [
            remote(ref.at[slot_id], ref.at[slot_id], gsend.at[first + k], grecv.at[first + k], peer)
            for k, peer in enumerate(peers)
        ]
        for copy in copies:
            copy.start()
        return copies

    copies = exchange(r1, z, zs, 0)
    err_col = jnp.sum(square, axis=1, keepdims=True) * (1.0 / C) * lw_col
    for copy in copies:
        copy.wait()
    for zz in range(NZ):
        r4[core, x, y, 2 * zz : 2 * zz + 2, :] = r1[zz, 0:2, :]
    for copy in exchange(r4.at[core, x], y, ys, 7):
        copy.wait()
    for copy in exchange(r4.at[core], x, xs, 14):
        copy.wait()
    for copy in exchange(r4, core, cs, 17):
        copy.wait()

    values = jnp.transpose(r4[...].reshape(1024, 128))
    high = values.astype(BF16)
    rest = values - high.astype(F32)
    mid = rest.astype(BF16)
    low = (rest - mid.astype(F32)).astype(BF16)
    three = jnp.concatenate([high, mid, low], axis=0)
    for blk in range(4):
        part = jnp.dot(three, pt[:, 256 * blk : 256 * (blk + 1)], preferred_element_type=F32)
        es[:, 256 * blk : 256 * (blk + 1)] = part[:128] + part[128:256] + part[256:]

    def fold(value):
        total = value[:, 0:128]
        for blk in range(1, 8):
            total = total + value[:, 128 * blk : 128 * (blk + 1)]
        total = jnp.sum(total, axis=0, keepdims=True)
        total = jnp.broadcast_to(total, (8, 128))
        total = total + pltpu.roll(total, 64, 1)
        return total + pltpu.roll(total, 32, 1)

    points = float(NPTS // 2 * 32)
    count = jnp.broadcast_to(small[8:9, :], (8, 128))
    weight = jnp.broadcast_to(small[9:10, :], (8, 128))

    def lanes(thresh):
        return jnp.concatenate([thresh[0:1, :]] * 8, axis=1)

    thresh = 2.0 * fold(es[...]) / points

    def iterate(_, thresh):
        half = (es[...] - lanes(thresh)) * (0.5 / SMOOTH)
        tangent = jnp.tanh(half)
        above = 0.5 * (fold(tangent) + points)
        spread = 0.25 * fold(1.0 - tangent * tangent)
        return thresh + jnp.clip(
            DAMPING * SMOOTH * (above - count) / (spread + 1.0), -STEP_LIMIT, STEP_LIMIT
        )

    thresh = lax.fori_loop(0, ITERS, iterate, thresh)

    numbers = small[0:8, :]
    ratio = weight / count
    half_rows = lax.broadcasted_iota(jnp.int32, (NPTS, 1), 0) < NPTS // 2
    own_thresh, own_ratio = [], []
    for t in range(2):
        mine = numbers == (lat * 64 + lon * 2 + t).astype(F32)
        for source, sink in ((thresh, own_thresh), (ratio, own_ratio)):
            picked = jnp.where(mine, source, 0.0)
            sink.append(jnp.sum(jnp.sum(picked, axis=0, keepdims=True), axis=1, keepdims=True))
    my_thresh = jnp.where(half_rows, own_thresh[0], own_thresh[1])
    my_ratio = jnp.where(half_rows, own_ratio[0], own_ratio[1])
    sig = 1.0 / (1.0 + jnp.exp((my_thresh - err_col) * (1.0 / SMOOTH)))
    d_err = my_ratio * sig * lw_col
    gp = ((d_err * (2.0 / C)) * ds_ref[...]).astype(BF16)
    for t in range(2):
        piece = gp[t * 128 : (t + 1) * 128, :].reshape(ROWS, 16, C)
        pad[1 : 1 + ROWS, 8 + 16 * t : 24 + 16 * t, :] = piece.astype(F32)
        rowbuf[1, 0, 16 * t : 16 * (t + 1), :] = piece[0]
        rowbuf[1, 1, 16 * t : 16 * (t + 1), :] = piece[ROWS - 1]
    pack(1)
    halo = halo_copies(1)
    for copy in halo:
        copy.start()

    gb_out[...] = jnp.sum(gp.astype(F32), axis=0, keepdims=True)
    for a in range(3):
        for b in range(3):
            k = 3 * a + b
            gk_out[k * C : (k + 1) * C, :] = lax.dot_general(
                patch(a, b), gp, (((0,), (0,)), ((), ())), preferred_element_type=F32
            )

    scaled = (es[...] - lanes(thresh)) * (1.0 / SMOOTH)
    soft = jnp.maximum(scaled, 0.0) + jnp.log1p(jnp.exp(-jnp.abs(scaled)))
    rl_out[...] = (thresh + SMOOTH * fold(soft) / count)[0:1, :]

    for copy in halo:
        copy.wait()
    place(1)
    total = jnp.zeros((NPTS, C), F32)
    for a in range(3):
        for b in range(3):
            k = 3 * a + b
            total = total + lax.dot_general(
                patch(2 - a, 2 - b), w[k * C : (k + 1) * C, :],
                (((1,), (1,)), ((), ())), preferred_element_type=F32,
            )
    total = total.astype(BF16)
    for t in range(2):
        gf_out[:, 16 * t : 16 * (t + 1), :] = total[t * 128 : (t + 1) * 128].reshape(ROWS, 16, C)


def on_device(fields, kernel, bias, target, tile_list, tail_count, region_weight):
    nlat = NLAT * ROWS
    lat_w = jnp.asarray(
        np.cos(np.pi * (np.arange(nlat) + 0.5) / nlat - np.pi / 2).astype(np.float32)
    )
    order = tile_list.reshape(NREG, -1).T.reshape(8, 128).astype(F32)
    small = jnp.concatenate(
        [
            order,
            jnp.tile(tail_count.astype(F32), 4)[None],
            jnp.tile(region_weight, 4)[None],
            jnp.zeros((6, 128), F32),
        ],
        axis=0,
    )
    vmem = pl.BlockSpec(memory_space=pltpu.VMEM)
    dma = pltpu.SemaphoreType.DMA
    gf, gk, gb, rl = pl.pallas_call(
        body,
        out_shape=(
            jax.ShapeDtypeStruct((ROWS, COLS, C), BF16),
            jax.ShapeDtypeStruct((9 * C, C), F32),
            jax.ShapeDtypeStruct((1, C), F32),
            jax.ShapeDtypeStruct((1, 128), F32),
        ),
        in_specs=[vmem] * 5 + [pl.BlockSpec(memory_space=pltpu.SMEM)],
        out_specs=(vmem,) * 4,
        scratch_shapes=[
            pltpu.VMEM((ROWS + 2, 48, C), F32),
            pltpu.VMEM((3, 2, ROWS + 2, 16, C), BF16),
            pltpu.VMEM((2, 2, ROWS, C), F32),
            pltpu.VMEM((2, 2, COLS, C), BF16),
            pltpu.VMEM((2, 6, ROWS, C), F32),
            pltpu.VMEM((2, 2, COLS, C), BF16),
            pltpu.VMEM((NPTS, C), F32),
            pltpu.VMEM((NZ, 8, 128), F32),
            pltpu.VMEM((2, NX, NY, 16, 128), F32),
            pltpu.VMEM((1024, 1024), BF16),
            pltpu.VMEM((128, 1024), F32),
            dma((2, 8)), dma((2, 8)), dma((18,)), dma((18,)), dma((1,)), dma((1,)),
        ],
        compiler_params=pltpu.CompilerParams(
            collective_id=0, has_side_effects=True, vmem_limit_bytes=48 * 1024 * 1024
        ),
        name="layer",
    )(fields, kernel.reshape(9 * C, C), bias.reshape(1, C), target, small, lat_w)
    gk, gb = lax.psum((gk, gb), ("lat", "lon"))
    return gf, gk.astype(BF16).reshape(3, 3, C, C), gb.reshape(C), rl[0, :NREG]


def solution(mesh):
    placed = (P("lat", "lon", None), P(), P(), P("lat", "lon", None), P(), P(), P())
    return jax.shard_map(
        on_device,
        mesh=mesh,
        in_specs=placed,
        out_specs=(P("lat", "lon", None), P(), P(), P()),
        check_vma=False,
    )
```

time: 843 us -> 165 us (0.20); the launches traced: 833 us -> 164 us
  blocking collectives: 785 us -> 107 us
  Pallas kernels: 0 us -> 49 us
  starting transfers between devices: 24.7 us -> 0 us
  matrix products: 10.3 us -> 0 us
    psum x8 -> x1, blocking collectives: 785 us -> 107 us  [on_device(): gk, gb = lax.psum((gk, gb), ('lat', 'lon'))]
    pallas_call x0 -> x1, Pallas kernels: none -> 49 us  [on_device(): pl.pallas_call(body, out_shape=(jax.ShapeDtypeStruct((ROWS, COLS, C), BF1...]
    ppermute x8 -> x0, starting transfers between devices: 24.7 us -> none  [the longest x4 14 us: with_halo(): lax.ppermute(tail, axis, [(i, (i + 1) % count) for i in range(ends)])]
    dot_general x49 -> x0, matrix products: 10.3 us -> none  [the longest x9 2.82 us: on_device(): pre = pre + jnp.dot(patch, kernel[a, b], preferred_element_type=jnp.float32)]
  transfers between devices with their start and end apart: 8 -> 0, of which waited for: 2 -> 0; matrix products, arithmetic and copies ran while one was open for 0% -> 0% of each run, Pallas kernels for 0% -> 0%
where the time goes in v1:
time: 165 us; the launch traced here: 164 us
  blocking collectives  107 us (65%)
  Pallas kernels  49 us (30%)
  local copies, waits for them, and re-layouts  6.71 us (4%)
    psum x1, blocking collectives, on_device(): gk, gb = lax.psum((gk, gb), ('lat', 'lon'))  107 us
    pallas_call x1, Pallas kernels, on_device(): pl.pallas_call(body, out_shape=(jax.ShapeDtypeStruct((ROWS, COLS, C), BF1...  49 us
    unnamed x11, local copies, waits for them, and re-layouts  5.07 us

profile of v1, /device:TPU:1, one launch (start us, length us, event | category | flops | bytes accessed | tf_op | source)
XLA Modules:
  0.0 164.5 jit_solution(2975156400726239305)
XLA Ops:
  0.6 0.7 convert_element_type.22
  1.3 0.1 pad.3.clone
  1.4 0.1 broadcast_in_dim_tile.6
  1.5 0.7 tile.5
  2.1 0.1 broadcast_in_dim_tile.7
  2.2 0.7 convert_element_type.18
  2.9 0.1 convert_element_type.19
  3.0 0.1 copy.12
  3.0 0.1 convert_element_type.21
  3.1 0.1 maximum_maximum_fusion.small
  3.2 0.0 copy-start
  3.2 1.3 copy-done
  4.5 0.0 copy-start.1
  4.5 0.9 copy-done.1
  5.4 0.0 copy-start.2
  5.4 0.9 copy-done.2
  6.3 0.0 copy-start.3
  6.3 0.7 copy-done.3
  7.0 0.0 copy-start.4
  7.0 0.7 copy-done.4
  7.6 49.0 %layer.1 = (bf16[8,32,256]{2,1,0:T(8,128)(2,1)S(1)}, f32[2304,256]{1,0:T(8,128)S(1)}, f32[1,256]{1,0:T(1,128)S(1)}, f32[1,128]{1,0:T(1,128)S(1)}) custom-call(bf16[8,32,256]{2,1,0:T(8,128)(2,1)S(1)} %copy-done.1, bf16[2304,256]{1,0:T(8,128)(2,1)S(1)} %bitcast.7, f32[1,256]{1,0:T(1,128)S(1)} %bitcast.8, bf16[8,32,256]{2,1,0:T(8,128)(2,1)S(1)} %copy-done.2, ...), custom_call_target="tpu_custom_call" | custom-call | tf_op jit(solution)/shard_map/layer/pallas_call | solution.py:302
  56.6 0.5 slice_bitcast_fusion
  57.1 106.7 %all-reduce.2 = (bf16[2304,256]{1,0:T(8,128)(2,1)}, f32[256]{0:T(256)}) all-reduce(f32[2304,256]{1,0:T(8,128)S(1)} %get-tuple-element.9, f32[256]{0:T(256)S(1)} %bitcast.9), channel_id=1, replica_groups=mesh['lat'=16,'lon'=32] {'lat','lon'}, use_global_device_ids=true, to_apply=%region_0.0 | all-reduce | flops 590080 | bytes 3540992 | tf_op jit(solution)/shard_map/psum | solution.py:331
  163.8 0.7 copy.18
  (2 shorter events, 0.0 us)
Async XLA Ops:
  3.2 1.3 copy-start
  4.5 0.9 copy-start.1
  5.4 0.9 copy-start.2
  6.3 0.7 copy-start.3
  7.0 0.7 copy-start.4

commit v2 on v1

--- a/solution.py
+++ b/solution.py
@@ -2,7 +2,6 @@
 
 import jax
 import jax.numpy as jnp
-import numpy as np
 from jax import lax
 from jax.experimental import pallas as pl
 from jax.experimental.pallas import tpu as pltpu
@@ -56,11 +55,23 @@
     return zs, ys, xs, [device_at(x, y, z, 1 - core)]
 
 
-def body(fields, w, bias, target, small, lw,
+def body(fields_hbm, w_hbm, bias_hbm, target_hbm, list_hbm, tail_hbm, weight_hbm,
          gf_out, gk_out, gb_out, rl_out,
+         fields, w, bias, target, tiles_i, tail_i, weight_f, small, lwc,
          pad, shifted, colbuf, rowbuf, colrec, rowrec, ds_ref, r1, r4, pt, es,
-         hsend, hrecv, gsend, grecv, zsend, zrecv):
+         gk, cbuf, crec, hx, hy, hz, sx, sy, sz, rx, ry, rz,
+         hx2, sx2, rx2, sy2, ry2, sz2, rz2, ex, ey, ez, fy, fz, gb0, gbx, gby, gbz,
+         lsem, hsend, hrecv, gsend, grecv, asend, arecv):
     lat, lon, x, y, z, core = position()
+    loads = [
+        pltpu.make_async_copy(src, dst, lsem.at[n])
+        for n, (src, dst) in enumerate((
+            (fields_hbm, fields), (list_hbm, tiles_i), (tail_hbm, tail_i),
+            (weight_hbm, weight_f), (w_hbm, w), (bias_hbm, bias), (target_hbm, target),
+        ))
+    ]
+    for load in loads:
+        load.start()
     zs, ys, xs, cs = line_peers(x, y, z, core)
     halos = halo_peers(lat, lon)
 
@@ -116,6 +127,7 @@
         parts = [shifted[b, t, a : a + ROWS].reshape(NPTS // 2, C) for t in range(2)]
         return jnp.concatenate(parts, axis=0)
 
+    loads[0].wait()
     for r in range(ROWS):
         pad[1 + r, 8 : 8 + COLS, :] = fields[r].astype(F32)
     pack(0)
@@ -126,10 +138,49 @@
     for copy in halo:
         copy.start()
 
+    for load in loads[1:4]:
+        load.wait()
+    lane = lax.broadcasted_iota(jnp.int32, (8, 128), 1)
+    row = lax.broadcasted_iota(jnp.int32, (8, 128), 0)
+    wide = jnp.concatenate([tiles_i[...].astype(F32), jnp.zeros((120, 128), F32)], axis=0)
+    wide = jnp.transpose(wide)
+    src_b = lax.broadcasted_iota(jnp.int32, (128, 128), 0)
+    dst_r = lax.broadcasted_iota(jnp.int32, (128, 128), 1) & 31
+    by_member = jnp.zeros((32, 128), F32)
+    for q in range(4):
+        pick = jnp.where(4 * src_b + q == dst_r, 1.0, 0.0)
+        by_member = by_member + jnp.dot(
+            wide[32 * q : 32 * (q + 1), :], pick,
+            precision=lax.Precision.HIGHEST, preferred_element_type=F32,
+        )
+    quarter = lane[0:1, :] >> 5
+    for blk in range(8):
+        line = by_member[4 * blk : 4 * blk + 1, :]
+        for j in range(1, 4):
+            line = jnp.where(quarter == j, by_member[4 * blk + j : 4 * blk + j + 1, :], line)
+        small[blk : blk + 1, :] = line
+    small[8:16, :] = jnp.zeros((8, 128), F32)
+    small[8:9, 0:NREG] = tail_i[...].astype(F32)
+    small[9:10, 0:NREG] = weight_f[...]
+    tails = small[8:16, :]
+    tails = tails + pltpu.roll(tails, 64, 1)
+    small[8:16, :] = tails + pltpu.roll(tails, 32, 1)
+
+    def lat_weight(row_in_band):
+        ids = (row_in_band + lat * ROWS).astype(F32)
+        return jnp.cos(jnp.pi * (ids + 0.5) / (NLAT * ROWS) - jnp.pi / 2)
+
+    lw8 = lat_weight(row)
+    for i in range(ROWS):
+        for t in range(2):
+            at = 128 * t + 16 * i
+            lwc[at : at + 16, :] = jnp.broadcast_to(lw8[i : i + 1, :], (16, 128))
+    lw_row = lat_weight((lax.broadcasted_iota(jnp.int32, (1, NPTS), 1) >> 4) & 7)
+
     slot = lax.broadcasted_iota(jnp.int32, (1024, 128), 0)
-    st, sz, sy = slot & 1, (slot >> 1) & 7, (slot >> 4) & 7
-    sx, sc = (slot >> 7) & 3, slot >> 9
-    tile = ((sy >> 2) * 8 + sz) * 64 + (sx * 8 + (sy & 3) * 2 + sc) * 2 + st
+    at_t, at_z, at_y = slot & 1, (slot >> 1) & 7, (slot >> 4) & 7
+    at_x, at_c = (slot >> 7) & 3, slot >> 9
+    tile = ((at_y >> 2) * 8 + at_z) * 64 + (at_x * 8 + (at_y & 3) * 2 + at_c) * 2 + at_t
     tile = tile.astype(F32)
     for blk in range(8):
         pt[:, 128 * blk : 128 * (blk + 1)] = jnp.where(
@@ -140,6 +191,8 @@
         copy.wait()
     place(0)
 
+    for load in loads[4:]:
+        load.wait()
     pre = jnp.zeros((NPTS, C), F32)
     for a in range(3):
         for b in range(3):
@@ -155,13 +208,7 @@
     diff = act - aim.astype(F32)
     ds_ref[...] = diff * slope
     square = diff * diff
-    prow = (lax.broadcasted_iota(jnp.int32, (1, NPTS), 1) >> 4) & 7
-    pcol = (lax.broadcasted_iota(jnp.int32, (NPTS, 1), 0) >> 4) & 7
-    lw_row, lw_col = jnp.zeros((1, NPTS), F32), jnp.zeros((NPTS, 1), F32)
-    for i in range(ROWS):
-        weight = lw[lat * ROWS + i]
-        lw_row = jnp.where(prow == i, weight, lw_row)
-        lw_col = jnp.where(pcol == i, weight, lw_col)
+    lw_col = lwc[:, 0:1]
     err_row = lax.dot_general(
         jnp.ones((8, C), F32), square, (((1,), (1,)), ((), ())),
         precision=lax.Precision.HIGHEST, preferred_element_type=F32,
@@ -254,20 +301,48 @@
     for copy in halo:
         copy.start()
 
-    gb_out[...] = jnp.sum(gp.astype(F32), axis=0, keepdims=True)
     for a in range(3):
         for b in range(3):
             k = 3 * a + b
-            gk_out[k * C : (k + 1) * C, :] = lax.dot_general(
+            tap = lax.dot_general(
                 patch(a, b), gp, (((0,), (0,)), ((), ())), preferred_element_type=F32
             )
-
-    scaled = (es[...] - lanes(thresh)) * (1.0 / SMOOTH)
-    soft = jnp.maximum(scaled, 0.0) + jnp.log1p(jnp.exp(-jnp.abs(scaled)))
-    rl_out[...] = (thresh + SMOOTH * fold(soft) / count)[0:1, :]
-
-    for copy in halo:
-        copy.wait()
+            if k == 4:
+                gk[0, 1024:1152, :] = tap[0:128]
+                gk[1, 0:128, :] = tap[128:256]
+            elif k < 4:
+                gk[0, k * C : (k + 1) * C, :] = tap
+            else:
+                at = k * C - 1152
+                gk[1, at : at + C, :] = tap
+    gb0[core] = jnp.sum(gp.astype(F32), axis=0, keepdims=True)
+
+    used = [0]
+
+    def send(src, dst, peer):
+        n = used[0]
+        used[0] += 1
+        copy = remote(src, dst, asend.at[n], arecv.at[n], peer)
+        copy.start()
+        return copy
+
+    def wait(copies):
+        for copy in copies:
+            copy.wait()
+
+    def share(ref, slot_id, peers):
+        return [send(ref.at[slot_id], ref.at[slot_id], peer) for peer in peers]
+
+    def scatter(src, dst, me, count, peers):
+        return [
+            send(src.at[(me + k) % count], dst.at[k - 1], peer)
+            for k, peer in zip(range(1, count), peers)
+        ]
+
+    cbuf[...] = gk[1 - core].astype(BF16)
+    copies = [send(cbuf, crec, cs[0])] + share(gb0, core, cs)
+
+    wait(halo)
     place(1)
     total = jnp.zeros((NPTS, C), F32)
     for a in range(3):
@@ -281,55 +356,128 @@
     for t in range(2):
         gf_out[:, 16 * t : 16 * (t + 1), :] = total[t * 128 : (t + 1) * 128].reshape(ROWS, 16, C)
 
+    wait(copies)
+    for parts, sends, base, size, pieces in (
+        (hx, sx, 0, 128, NX), (hy, sy, 512, 48, NY), (hz, sz, 896, 32, NZ),
+    ):
+        for n in range(pieces):
+            at = base + n * size
+            chunk = gk[core, at : at + size, :] + crec[at : at + size, :].astype(F32)
+            parts[n] = chunk
+            sends[n] = chunk.astype(BF16)
+    gbx[x] = gb0[0] + gb0[1]
+
+    copies = (
+        scatter(sx, rx, x, NX, xs) + scatter(sy, ry, y, NY, ys) + scatter(sz, rz, z, NZ, zs)
+        + share(gbx, x, xs)
+    )
+
+    scaled = (es[...] - lanes(thresh)) * (1.0 / SMOOTH)
+    soft = jnp.maximum(scaled, 0.0) + jnp.log1p(jnp.exp(-jnp.abs(scaled)))
+    rl_out[...] = (thresh + SMOOTH * fold(soft) / count)[0:1, :]
+
+    wait(copies)
+
+    def gathered(own, received):
+        for n in range(received.shape[0]):
+            own = own + received[n].astype(F32)
+        return own
+
+    def in_order(ref):
+        value = ref[0].astype(F32)
+        for n in range(1, ref.shape[0]):
+            value = value + ref[n].astype(F32)
+        return value
+
+    part = gathered(hx[x], rx)
+    for n in range(NY):
+        hx2[n] = part[16 * n : 16 * (n + 1), :]
+        sx2[n] = part[16 * n : 16 * (n + 1), :].astype(BF16)
+    hy[y] = gathered(hy[y], ry)
+    for n in range(NZ):
+        sy2[n, 0:6, :] = hy[y, 6 * n : 6 * n + 6, :]
+        sy2[n, 6:8, :] = jnp.zeros((2, C), F32)
+    part = gathered(hz[z], rz)
+    for n in range(NX):
+        sz2[n] = part[8 * n : 8 * (n + 1), :]
+    gby[y] = in_order(gbx)
+    wait(
+        scatter(sx2, rx2, y, NY, ys) + scatter(sy2, ry2, z, NZ, zs) + scatter(sz2, rz2, x, NX, xs)
+        + share(gby, y, ys)
+    )
+
+    ex[z] = gathered(hx2[y], rx2).astype(BF16)
+    ey[x] = gathered(sy2[z], ry2)
+    ez[y] = gathered(sz2[x], rz2)
+    gbz[z] = in_order(gby)
+    wait(share(ex, z, zs) + share(ey, x, xs) + share(ez, y, ys) + share(gbz, z, zs))
+    gb_out[...] = in_order(gbz)
+
+    at = pl.multiple_of(128 * x + 16 * y, 16)
+    gk_out[core, pl.ds(at, 16), :] = in_order(ex).astype(BF16)
+    fy[z] = in_order(ey)
+    fz[x] = in_order(ez)
+    mine = gk_out.at[core, pl.ds(at, 16)]
+    wait([send(mine, mine, peer) for peer in ys] + share(fy, z, zs) + share(fz, x, xs))
+    for n in range(NZ):
+        hy[y, 6 * n : 6 * n + 6, :] = fy[n, 0:6, :]
+    at_x = pl.multiple_of(128 * x, 128)
+    at_y = pl.multiple_of(512 + 48 * y, 16)
+    at_z = pl.multiple_of(896 + 32 * z, 16)
+    gk_out[core, pl.ds(at_y, 48), :] = hy[y].astype(BF16)
+    gk_out[core, pl.ds(at_z, 32), :] = fz[...].reshape(32, C).astype(BF16)
+    copies = []
+    for at, size, peers in ((at_x, 128, xs), (at_y, 48, ys), (at_z, 32, zs)):
+        mine = gk_out.at[core, pl.ds(at, size)]
+        copies += [send(mine, mine, peer) for peer in peers]
+    wait(copies)
+    wait(share(gk_out, core, cs))
+
 
 def on_device(fields, kernel, bias, target, tile_list, tail_count, region_weight):
-    nlat = NLAT * ROWS
-    lat_w = jnp.asarray(
-        np.cos(np.pi * (np.arange(nlat) + 0.5) / nlat - np.pi / 2).astype(np.float32)
-    )
-    order = tile_list.reshape(NREG, -1).T.reshape(8, 128).astype(F32)
-    small = jnp.concatenate(
-        [
-            order,
-            jnp.tile(tail_count.astype(F32), 4)[None],
-            jnp.tile(region_weight, 4)[None],
-            jnp.zeros((6, 128), F32),
-        ],
-        axis=0,
-    )
     vmem = pl.BlockSpec(memory_space=pltpu.VMEM)
     dma = pltpu.SemaphoreType.DMA
+    v = pltpu.VMEM
     gf, gk, gb, rl = pl.pallas_call(
         body,
         out_shape=(
             jax.ShapeDtypeStruct((ROWS, COLS, C), BF16),
-            jax.ShapeDtypeStruct((9 * C, C), F32),
+            jax.ShapeDtypeStruct((2, 1152, C), BF16),
             jax.ShapeDtypeStruct((1, C), F32),
             jax.ShapeDtypeStruct((1, 128), F32),
         ),
-        in_specs=[vmem] * 5 + [pl.BlockSpec(memory_space=pltpu.SMEM)],
+        in_specs=[pl.BlockSpec(memory_space=pl.ANY)] * 7,
         out_specs=(vmem,) * 4,
         scratch_shapes=[
-            pltpu.VMEM((ROWS + 2, 48, C), F32),
-            pltpu.VMEM((3, 2, ROWS + 2, 16, C), BF16),
-            pltpu.VMEM((2, 2, ROWS, C), F32),
-            pltpu.VMEM((2, 2, COLS, C), BF16),
-            pltpu.VMEM((2, 6, ROWS, C), F32),
-            pltpu.VMEM((2, 2, COLS, C), BF16),
-            pltpu.VMEM((NPTS, C), F32),
-            pltpu.VMEM((NZ, 8, 128), F32),
-            pltpu.VMEM((2, NX, NY, 16, 128), F32),
-            pltpu.VMEM((1024, 1024), BF16),
-            pltpu.VMEM((128, 1024), F32),
-            dma((2, 8)), dma((2, 8)), dma((18,)), dma((18,)), dma((1,)), dma((1,)),
+            v((ROWS, COLS, C), BF16), v((9 * C, C), BF16), v((1, C), F32), v((ROWS, COLS, C), BF16),
+            v((8, 128), jnp.int32), v((1, NREG), jnp.int32), v((1, NREG), F32),
+            v((16, 128), F32), v((NPTS, 128), F32),
+            v((ROWS + 2, 48, C), F32), v((3, 2, ROWS + 2, 16, C), BF16),
+            v((2, 2, ROWS, C), F32), v((2, 2, COLS, C), BF16),
+            v((2, 6, ROWS, C), F32), v((2, 2, COLS, C), BF16),
+            v((NPTS, C), F32), v((NZ, 8, 128), F32), v((2, NX, NY, 16, 128), F32),
+            v((1024, 1024), BF16), v((128, 1024), F32),
+            v((2, 1152, C), F32), v((1152, C), BF16), v((1152, C), BF16),
+            v((NX, 128, C), F32), v((NY, 48, C), F32), v((NZ, 32, C), F32),
+            v((NX, 128, C), BF16), v((NY, 48, C), BF16), v((NZ, 32, C), BF16),
+            v((NX - 1, 128, C), BF16), v((NY - 1, 48, C), BF16), v((NZ - 1, 32, C), BF16),
+            v((NY, 16, C), F32), v((NY, 16, C), BF16), v((NY - 1, 16, C), BF16),
+            v((NZ, 8, C), F32), v((NZ - 1, 8, C), F32),
+            v((NX, 8, C), F32), v((NX - 1, 8, C), F32),
+            v((NZ, 16, C), BF16), v((NX, 8, C), F32), v((NY, 8, C), F32),
+            v((NZ, 8, C), F32), v((NX, 8, C), F32),
+            v((2, 1, C), F32), v((NX, 1, C), F32), v((NY, 1, C), F32), v((NZ, 1, C), F32),
+            dma((7,)), dma((2, 8)), dma((2, 8)), dma((18,)), dma((18,)), dma((105,)), dma((105,)),
         ],
         compiler_params=pltpu.CompilerParams(
-            collective_id=0, has_side_effects=True, vmem_limit_bytes=48 * 1024 * 1024
+            collective_id=0, has_side_effects=True, vmem_limit_bytes=60 * 1024 * 1024
         ),
         name="layer",
-    )(fields, kernel.reshape(9 * C, C), bias.reshape(1, C), target, small, lat_w)
-    gk, gb = lax.psum((gk, gb), ("lat", "lon"))
-    return gf, gk.astype(BF16).reshape(3, 3, C, C), gb.reshape(C), rl[0, :NREG]
+    )(
+        fields, kernel.reshape(9 * C, C), bias.reshape(1, C), target,
+        tile_list.reshape(8, 128), tail_count.reshape(1, NREG), region_weight.reshape(1, NREG),
+    )
+    return gf, gk.reshape(3, 3, C, C), gb.reshape(C), rl[0, :NREG]
 
 
 def solution(mesh):

time: 165 us -> 90.6 us (0.55)
  blocking collectives: 107 us -> 0 us
  Pallas kernels: 49 us -> 84.2 us
    psum x1 -> x0, blocking collectives: 107 us -> none  [on_device(): gk, gb = lax.psum((gk, gb), ('lat', 'lon'))]
    pallas_call x1, Pallas kernels: 49 us -> 84.2 us  [on_device(): pl.pallas_call(body, out_shape=(jax.ShapeDtypeStruct((ROWS, COLS, C), BF1...]
    unnamed x11 -> x5, local copies, waits for them, and re-layouts: 5.07 us -> 4.49 us
where the time goes in v2:
time: 90.6 us; the launch traced here: 90.4 us
  Pallas kernels  84.2 us (93%)
  local copies, waits for them, and re-layouts  5.61 us (6%)
    pallas_call x1, Pallas kernels, on_device(): pl.pallas_call(body, out_shape=(jax.ShapeDtypeStruct((ROWS, COLS, C), BF1...  84.2 us
    unnamed x5, local copies, waits for them, and re-layouts  4.49 us

profile of v2, /device:TPU:1, one launch (start us, length us, event | category | flops | bytes accessed | tf_op | source)
XLA Modules:
  0.0 90.4 jit_solution(3869390992189290184)
XLA Ops:
  0.6 84.2 %layer.1 = (bf16[8,32,256]{2,1,0:T(8,128)(2,1)}, bf16[2,1152,256]{2,1,0:T(8,128)(2,1)}, f32[1,256]{1,0:T(1,128)}, f32[1,128]{1,0:T(1,128)}) custom-call(bf16[8,32,256]{2,1,0:T(8,128)(2,1)} %fields_hbm.1, bf16[2304,256]{1,0:T(8,128)(2,1)} %bitcast.9, f32[1,256]{1,0:T(1,128)} %bitcast.13, bf16[8,32,256]{2,1,0:T(8,128)(2,1)} %target_hbm.1, s32[8,128]{1,0:T(8,128)} %bitcast.11, ...), custom_call_target="tpu_custom_call" | custom-call | tf_op jit(solution)/shard_map/layer/pallas_call | solution.py:441
  84.8 1.1 %slice_bitcast_fusion = f32[32]{0:T(128)} fusion(f32[1,128]{1,0:T(1,128)} %get-tuple-element.11), kind=kLoop, calls=%fused_computation | loop fusion | bytes 256 | tf_op jit(solution)/shard_map/squeeze | solution.py:480
  85.9 1.6 %copy.14 = bf16[8,32,256]{2,1,0:T(8,128)(2,1)} copy(bf16[8,32,256]{2,1,0:T(8,128)(2,1)} %get-tuple-element.16) | data formatting | bytes 262144
  87.5 0.0 copy-start
  87.5 2.4 %copy.15 = bf16[3,3,256,256]{3,2,1,0:T(8,128)(2,1)} copy(bf16[3,3,256,256]{3,2,1,0:T(8,128)(2,1)} %bitcast.10) | data formatting | bytes 2359296
  89.9 0.0 copy-done
  89.9 0.6 copy.16
Async XLA Ops:
  87.5 2.4 %copy-start = (f32[1,256]{1,0:T(1,128)S(1)}, f32[1,256]{1,0:T(1,128)}, u32[]{:S(2)}) copy-start(f32[1,256]{1,0:T(1,128)} %get-tuple-element.10) | copy-start | bytes 3076

commit v3 on v2

--- a/solution.py
+++ b/solution.py
@@ -58,7 +58,7 @@
 def body(fields_hbm, w_hbm, bias_hbm, target_hbm, list_hbm, tail_hbm, weight_hbm,
          gf_out, gk_out, gb_out, rl_out,
          fields, w, bias, target, tiles_i, tail_i, weight_f, small, lwc,
-         pad, shifted, colbuf, rowbuf, colrec, rowrec, ds_ref, r1, r4, pt, es,
+         pad, shifted, turned, colbuf, rowbuf, colrec, rowrec, ds_ref, r1, r4, pt, es,
          gk, cbuf, crec, hx, hy, hz, sx, sy, sz, rx, ry, rz,
          hx2, sx2, rx2, sy2, ry2, sz2, rz2, ex, ey, ez, fy, fz, gb0, gbx, gby, gbz,
          lsem, hsend, hrecv, gsend, grecv, asend, arecv):
@@ -225,17 +225,27 @@
             copy.start()
         return copies
 
+    def turn(taps):
+        for k in taps:
+            turned[k] = jnp.transpose(patch(k // 3, k % 3))
+
     copies = exchange(r1, z, zs, 0)
     err_col = jnp.sum(square, axis=1, keepdims=True) * (1.0 / C) * lw_col
+    turn(range(4))
     for copy in copies:
         copy.wait()
     for zz in range(NZ):
         r4[core, x, y, 2 * zz : 2 * zz + 2, :] = r1[zz, 0:2, :]
-    for copy in exchange(r4.at[core, x], y, ys, 7):
+    copies = exchange(r4.at[core, x], y, ys, 7)
+    turn(range(4, 9))
+    for copy in copies:
         copy.wait()
-    for copy in exchange(r4.at[core], x, xs, 14):
-        copy.wait()
-    for copy in exchange(r4, core, cs, 17):
+    copies = exchange(r4.at[core], x, xs, 14)
+    passed = exchange(r4.at[core], x, cs, 17)
+    for n, k in enumerate((1, 3, 2)):
+        copies[k - 1].wait()
+        passed += exchange(r4.at[core], (x + NX - k) % NX, cs, 18 + n)
+    for copy in passed:
         copy.wait()
 
     values = jnp.transpose(r4[...].reshape(1024, 128))
@@ -301,12 +311,11 @@
     for copy in halo:
         copy.start()
 
-    for a in range(3):
-        for b in range(3):
-            k = 3 * a + b
-            tap = lax.dot_general(
-                patch(a, b), gp, (((0,), (0,)), ((), ())), preferred_element_type=F32
-            )
+    gb0[core] = jnp.sum(gp.astype(F32), axis=0, keepdims=True)
+
+    def taps(which):
+        for k in which:
+            tap = jnp.dot(turned[k], gp, preferred_element_type=F32)
             if k == 4:
                 gk[0, 1024:1152, :] = tap[0:128]
                 gk[1, 0:128, :] = tap[128:256]
@@ -315,7 +324,6 @@
             else:
                 at = k * C - 1152
                 gk[1, at : at + C, :] = tap
-    gb0[core] = jnp.sum(gp.astype(F32), axis=0, keepdims=True)
 
     used = [0]
 
@@ -339,8 +347,38 @@
             for k, peer in zip(range(1, count), peers)
         ]
 
-    cbuf[...] = gk[1 - core].astype(BF16)
-    copies = [send(cbuf, crec, cs[0])] + share(gb0, core, cs)
+    spans = {"x": (0, 512), "y": (512, 896), "z": (896, 1152)}
+
+    def to_other_core(name):
+        low, high = spans[name]
+        cbuf[low:high, :] = gk[1 - core, low:high, :].astype(BF16)
+        return [send(cbuf.at[low:high], crec.at[low:high], cs[0])]
+
+    taps((2, 3, 6, 7))
+    paired_y = to_other_core("y")
+    taps((0, 1, 4, 5))
+    paired_x = to_other_core("x")
+    taps((8,))
+    paired_z = to_other_core("z") + share(gb0, core, cs)
+
+    def split(name, parts, sends, size):
+        for n in range(parts.shape[0]):
+            at = spans[name][0] + n * size
+            chunk = gk[core, at : at + size, :] + crec[at : at + size, :].astype(F32)
+            parts[n] = chunk
+            sends[n] = chunk.astype(BF16)
+
+    wait(paired_y)
+    split("y", hy, sy, 48)
+    first_y = scatter(sy, ry, y, NY, ys)
+    wait(paired_x)
+    split("x", hx, sx, 128)
+    first_x = scatter(sx, rx, x, NX, xs)
+    wait(paired_z)
+    split("z", hz, sz, 32)
+    first_z = scatter(sz, rz, z, NZ, zs)
+    gbx[x] = gb0[0] + gb0[1]
+    first_x += share(gbx, x, xs)
 
     wait(halo)
     place(1)
@@ -356,27 +394,9 @@
     for t in range(2):
         gf_out[:, 16 * t : 16 * (t + 1), :] = total[t * 128 : (t + 1) * 128].reshape(ROWS, 16, C)
 
-    wait(copies)
-    for parts, sends, base, size, pieces in (
-        (hx, sx, 0, 128, NX), (hy, sy, 512, 48, NY), (hz, sz, 896, 32, NZ),
-    ):
-        for n in range(pieces):
-            at = base + n * size
-            chunk = gk[core, at : at + size, :] + crec[at : at + size, :].astype(F32)
-            parts[n] = chunk
-            sends[n] = chunk.astype(BF16)
-    gbx[x] = gb0[0] + gb0[1]
-
-    copies = (
-        scatter(sx, rx, x, NX, xs) + scatter(sy, ry, y, NY, ys) + scatter(sz, rz, z, NZ, zs)
-        + share(gbx, x, xs)
-    )
-
     scaled = (es[...] - lanes(thresh)) * (1.0 / SMOOTH)
     soft = jnp.maximum(scaled, 0.0) + jnp.log1p(jnp.exp(-jnp.abs(scaled)))
-    rl_out[...] = (thresh + SMOOTH * fold(soft) / count)[0:1, :]
-
-    wait(copies)
+    rl_out[...] = (thresh + SMOOTH * fold(soft) / count)[0:1, 0:NREG]
 
     def gathered(own, received):
         for n in range(received.shape[0]):
@@ -389,49 +409,88 @@
             value = value + ref[n].astype(F32)
         return value
 
+    wait(first_x)
     part = gathered(hx[x], rx)
     for n in range(NY):
         hx2[n] = part[16 * n : 16 * (n + 1), :]
         sx2[n] = part[16 * n : 16 * (n + 1), :].astype(BF16)
+    gby[y] = in_order(gbx)
+    second_x = scatter(sx2, rx2, y, NY, ys) + share(gby, y, ys)
+
+    wait(first_z)
+    part = gathered(hz[z], rz)
+    for n in range(NX):
+        sz2[n] = part[8 * n : 8 * (n + 1), :]
+    second_z = scatter(sz2, rz2, x, NX, xs)
+
+    wait(first_y)
     hy[y] = gathered(hy[y], ry)
     for n in range(NZ):
         sy2[n, 0:6, :] = hy[y, 6 * n : 6 * n + 6, :]
         sy2[n, 6:8, :] = jnp.zeros((2, C), F32)
-    part = gathered(hz[z], rz)
-    for n in range(NX):
-        sz2[n] = part[8 * n : 8 * (n + 1), :]
-    gby[y] = in_order(gbx)
-    wait(
-        scatter(sx2, rx2, y, NY, ys) + scatter(sy2, ry2, z, NZ, zs) + scatter(sz2, rz2, x, NX, xs)
-        + share(gby, y, ys)
-    )
-
+    second_y = scatter(sy2, ry2, z, NZ, zs)
+
+    wait(second_x)
     ex[z] = gathered(hx2[y], rx2).astype(BF16)
+    gbz[z] = in_order(gby)
+    third_x = share(ex, z, zs) + share(gbz, z, zs)
+    wait(second_z)
+    ez[y] = gathered(sz2[x], rz2)
+    third_z = share(ez, y, ys)
+    wait(second_y)
     ey[x] = gathered(sy2[z], ry2)
-    ez[y] = gathered(sz2[x], rz2)
-    gbz[z] = in_order(gby)
-    wait(share(ex, z, zs) + share(ey, x, xs) + share(ez, y, ys) + share(gbz, z, zs))
-    gb_out[...] = in_order(gbz)
-
+    third_y = share(ey, x, xs)
+
+    wait(third_x)
     at = pl.multiple_of(128 * x + 16 * y, 16)
     gk_out[core, pl.ds(at, 16), :] = in_order(ex).astype(BF16)
+    mine = gk_out.at[core, pl.ds(at, 16)]
+    fourth_x = [send(mine, mine, peer) for peer in ys]
+    gb_out[...] = in_order(gbz)
+    wait(third_y)
     fy[z] = in_order(ey)
+    fourth_y = share(fy, z, zs)
+    wait(third_z)
     fz[x] = in_order(ez)
-    mine = gk_out.at[core, pl.ds(at, 16)]
-    wait([send(mine, mine, peer) for peer in ys] + share(fy, z, zs) + share(fz, x, xs))
+    fourth_z = share(fz, x, xs)
+
+    def spread_out(at, size, peers):
+        mine = gk_out.at[core, pl.ds(at, size)]
+        return [send(mine, mine, peer) for peer in peers]
+
+    def hand_over(name):
+        low, high = spans[name]
+        mine = gk_out.at[core, low:high]
+        return [send(mine, mine, cs[0])]
+
+    wait(fourth_z)
+    at_z = pl.multiple_of(896 + 32 * z, 16)
+    gk_out[core, pl.ds(at_z, 32), :] = fz[...].reshape(32, C).astype(BF16)
+    fifth_z = spread_out(at_z, 32, zs)
+    wait(fourth_y)
     for n in range(NZ):
         hy[y, 6 * n : 6 * n + 6, :] = fy[n, 0:6, :]
-    at_x = pl.multiple_of(128 * x, 128)
     at_y = pl.multiple_of(512 + 48 * y, 16)
-    at_z = pl.multiple_of(896 + 32 * z, 16)
     gk_out[core, pl.ds(at_y, 48), :] = hy[y].astype(BF16)
-    gk_out[core, pl.ds(at_z, 32), :] = fz[...].reshape(32, C).astype(BF16)
-    copies = []
-    for at, size, peers in ((at_x, 128, xs), (at_y, 48, ys), (at_z, 32, zs)):
-        mine = gk_out.at[core, pl.ds(at, size)]
-        copies += [send(mine, mine, peer) for peer in peers]
-    wait(copies)
-    wait(share(gk_out, core, cs))
+    fifth_y = spread_out(at_y, 48, ys)
+    wait(fourth_x)
+    fifth_x = spread_out(pl.multiple_of(128 * x, 128), 128, xs)
+    wait(fifth_z)
+    last = hand_over("z")
+    wait(fifth_x)
+    last += hand_over("x")
+    wait(fifth_y)
+    last += hand_over("y")
+    wait(last)
+
+
+def leave(gf, gk, gb, rl, gf_out, gk_out, gb_out, rl_out, sems):
+    pairs = ((gk, gk_out), (gf, gf_out), (gb, gb_out), (rl, rl_out))
+    copies = [pltpu.make_async_copy(a, b, sems.at[n]) for n, (a, b) in enumerate(pairs)]
+    for copy in copies:
+        copy.start()
+    for copy in copies:
+        copy.wait()
 
 
 def on_device(fields, kernel, bias, target, tile_list, tail_count, region_weight):
@@ -444,7 +503,7 @@
             jax.ShapeDtypeStruct((ROWS, COLS, C), BF16),
             jax.ShapeDtypeStruct((2, 1152, C), BF16),
             jax.ShapeDtypeStruct((1, C), F32),
-            jax.ShapeDtypeStruct((1, 128), F32),
+            jax.ShapeDtypeStruct((1, NREG), F32),
         ),
         in_specs=[pl.BlockSpec(memory_space=pl.ANY)] * 7,
         out_specs=(vmem,) * 4,
@@ -452,7 +511,7 @@
             v((ROWS, COLS, C), BF16), v((9 * C, C), BF16), v((1, C), F32), v((ROWS, COLS, C), BF16),
             v((8, 128), jnp.int32), v((1, NREG), jnp.int32), v((1, NREG), F32),
             v((16, 128), F32), v((NPTS, 128), F32),
-            v((ROWS + 2, 48, C), F32), v((3, 2, ROWS + 2, 16, C), BF16),
+            v((ROWS + 2, 48, C), F32), v((3, 2, ROWS + 2, 16, C), BF16), v((9, C, NPTS), BF16),
             v((2, 2, ROWS, C), F32), v((2, 2, COLS, C), BF16),
             v((2, 6, ROWS, C), F32), v((2, 2, COLS, C), BF16),
             v((NPTS, C), F32), v((NZ, 8, 128), F32), v((2, NX, NY, 16, 128), F32),
@@ -467,7 +526,7 @@
             v((NZ, 16, C), BF16), v((NX, 8, C), F32), v((NY, 8, C), F32),
             v((NZ, 8, C), F32), v((NX, 8, C), F32),
             v((2, 1, C), F32), v((NX, 1, C), F32), v((NY, 1, C), F32), v((NZ, 1, C), F32),
-            dma((7,)), dma((2, 8)), dma((2, 8)), dma((18,)), dma((18,)), dma((105,)), dma((105,)),
+            dma((7,)), dma((2, 8)), dma((2, 8)), dma((21,)), dma((21,)), dma((110,)), dma((110,)),
         ],
         compiler_params=pltpu.CompilerParams(
             collective_id=0, has_side_effects=True, vmem_limit_bytes=60 * 1024 * 1024
@@ -477,7 +536,17 @@
         fields, kernel.reshape(9 * C, C), bias.reshape(1, C), target,
         tile_list.reshape(8, 128), tail_count.reshape(1, NREG), region_weight.reshape(1, NREG),
     )
-    return gf, gk.reshape(3, 3, C, C), gb.reshape(C), rl[0, :NREG]
+    results = (gf, gk, gb, rl)
+    anywhere = pl.BlockSpec(memory_space=pl.ANY)
+    gf, gk, gb, rl = pl.pallas_call(
+        leave,
+        out_shape=[jax.ShapeDtypeStruct(r.shape, r.dtype) for r in results],
+        in_specs=[anywhere] * 4,
+        out_specs=[anywhere] * 4,
+        scratch_shapes=[dma((4,))],
+        name="leave",
+    )(*results)
+    return gf, gk.reshape(3, 3, C, C), gb.reshape(C), rl.reshape(NREG)
 
 
 def solution(mesh):

time: 90.6 us -> 120 us (1.32)
  Pallas kernels: 84.2 us -> 119 us
  local copies, waits for them, and re-layouts: 5.61 us -> 0 us
    pallas_call x0 -> x1, Pallas kernels: none -> 40.9 us  [on_device(): pl.pallas_call(leave, out_shape=[jax.ShapeDtypeStruct(r.shape, r.dtype) f...]
    pallas_call x1, Pallas kernels: 84.2 us -> 78.1 us  [on_device(): pl.pallas_call(body, out_shape=(jax.ShapeDtypeStruct((ROWS, COLS, C), BF1...]
    unnamed x5 -> x0, local copies, waits for them, and re-layouts: 4.49 us -> none
where the time goes in v3:
time: 120 us
  Pallas kernels  119 us (99%)
    pallas_call x1, Pallas kernels, on_device(): pl.pallas_call(body, out_shape=(jax.ShapeDtypeStruct((ROWS, COLS, C), BF1...  78.1 us
    pallas_call x1, Pallas kernels, on_device(): pl.pallas_call(leave, out_shape=[jax.ShapeDtypeStruct(r.shape, r.dtype) f...  40.9 us

profile of v3, /device:TPU:1, one launch (start us, length us, event | category | flops | bytes accessed | tf_op | source)
XLA Modules:
  0.0 119.6 jit_solution(12233649868376958118)
XLA Ops:
  0.6 78.1 %layer.1 = (bf16[8,32,256]{2,1,0:T(8,128)(2,1)}, bf16[2,1152,256]{2,1,0:T(8,128)(2,1)}, f32[1,256]{1,0:T(1,128)}, f32[1,32]{1,0:T(1,128)}) custom-call(bf16[8,32,256]{2,1,0:T(8,128)(2,1)} %fields_hbm.1, bf16[2304,256]{1,0:T(8,128)(2,1)} %bitcast.8, f32[1,256]{1,0:T(1,128)} %bitcast.10, bf16[8,32,256]{2,1,0:T(8,128)(2,1)} %target_hbm.1, s32[8,128]{1,0:T(8,128)} %bitcast.9, ...), custom_call_target="tpu_custom_call" | custom-call | tf_op jit(solution)/shard_map/layer/pallas_call | solution.py:500
  78.7 40.9 %leave.1 = (bf16[8,32,256]{2,1,0:T(8,128)(2,1)}, bf16[2,1152,256]{2,1,0:T(8,128)(2,1)}, f32[1,256]{1,0:T(1,128)}, f32[1,32]{1,0:T(1,128)}) custom-call(bf16[8,32,256]{2,1,0:T(8,128)(2,1)} %get-tuple-element.12.gf, bf16[2,1152,256]{2,1,0:T(8,128)(2,1)} %get-tuple-element.13.gk, f32[1,256]{1,0:T(1,128)} %get-tuple-element.14.gb, f32[1,32]{1,0:T(1,128)} %get-tuple-element.15.rl), custom_call_target="tpu_custom_call" | custom-call | tf_op jit(solution)/shard_map/leave/pallas_call | solution.py:541

commit v4 on v3

--- a/solution.py
+++ b/solution.py
@@ -484,12 +484,21 @@
     wait(last)
 
 
-def leave(gf, gk, gb, rl, gf_out, gk_out, gb_out, rl_out, sems):
-    pairs = ((gk, gk_out), (gf, gf_out), (gb, gb_out), (rl, rl_out))
-    copies = [pltpu.make_async_copy(a, b, sems.at[n]) for n, (a, b) in enumerate(pairs)]
-    for copy in copies:
+def leave(gf, gk, gb, rl, gf_out, gk_out, gb_out, rl_out, gf_v, gk_v, gb_v, rl_v, sems):
+    half = gk.shape[1] // 2
+    trips = [(gf, gf_v, gf_out), (gb, gb_v, gb_out), (rl, rl_v, rl_out)]
+    for h in range(2):
+        for low in (0, half):
+            span = pl.ds(low, half)
+            trips.append((gk.at[h, span], gk_v.at[h, span], gk_out.at[h, span]))
+    arrive = [pltpu.make_async_copy(a, b, sems.at[0, n]) for n, (a, b, _) in enumerate(trips)]
+    depart = [pltpu.make_async_copy(b, c, sems.at[1, n]) for n, (_, b, c) in enumerate(trips)]
+    for copy in arrive:
         copy.start()
-    for copy in copies:
+    for first, second in zip(arrive, depart):
+        first.wait()
+        second.start()
+    for copy in depart:
         copy.wait()
 
 
@@ -543,7 +552,7 @@
         out_shape=[jax.ShapeDtypeStruct(r.shape, r.dtype) for r in results],
         in_specs=[anywhere] * 4,
         out_specs=[anywhere] * 4,
-        scratch_shapes=[dma((4,))],
+        scratch_shapes=[pltpu.VMEM(r.shape, r.dtype) for r in results] + [dma((2, 7))],
         name="leave",
     )(*results)
     return gf, gk.reshape(3, 3, C, C), gb.reshape(C), rl.reshape(NREG)

time: 120 us -> 81 us (0.68)
  Pallas kernels: 119 us -> 80.2 us
    pallas_call x1, Pallas kernels: 40.9 us -> 2.17 us  [on_device(): pl.pallas_call(leave, out_shape=[jax.ShapeDtypeStruct(r.shape, r.dtype) f...]
where the time goes in v4:
time: 81 us; the launch traced here: 80.9 us
  Pallas kernels  80.2 us (99%)
    pallas_call x1, Pallas kernels, on_device(): pl.pallas_call(body, out_shape=(jax.ShapeDtypeStruct((ROWS, COLS, C), BF1...  78.1 us
    pallas_call x1, Pallas kernels, on_device(): pl.pallas_call(leave, out_shape=[jax.ShapeDtypeStruct(r.shape, r.dtype) f...  2.17 us

profile of v4, /device:TPU:1, one launch (start us, length us, event | category | flops | bytes accessed | tf_op | source)
XLA Modules:
  0.0 80.9 jit_solution(7176543475308691795)
XLA Ops:
  0.6 78.1 %layer.1 = (bf16[8,32,256]{2,1,0:T(8,128)(2,1)}, bf16[2,1152,256]{2,1,0:T(8,128)(2,1)}, f32[1,256]{1,0:T(1,128)}, f32[1,32]{1,0:T(1,128)}) custom-call(bf16[8,32,256]{2,1,0:T(8,128)(2,1)} %fields_hbm.1, bf16[2304,256]{1,0:T(8,128)(2,1)} %bitcast.8, f32[1,256]{1,0:T(1,128)} %bitcast.10, bf16[8,32,256]{2,1,0:T(8,128)(2,1)} %target_hbm.1, s32[8,128]{1,0:T(8,128)} %bitcast.9, ...), custom_call_target="tpu_custom_call" | custom-call | tf_op jit(solution)/shard_map/layer/pallas_call | solution.py:509
  78.7 2.2 %leave.1 = (bf16[8,32,256]{2,1,0:T(8,128)(2,1)}, bf16[2,1152,256]{2,1,0:T(8,128)(2,1)}, f32[1,256]{1,0:T(1,128)}, f32[1,32]{1,0:T(1,128)}) custom-call(bf16[8,32,256]{2,1,0:T(8,128)(2,1)} %get-tuple-element.12.gf, bf16[2,1152,256]{2,1,0:T(8,128)(2,1)} %get-tuple-element.13.gk, f32[1,256]{1,0:T(1,128)} %get-tuple-element.14.gb, f32[1,32]{1,0:T(1,128)} %get-tuple-element.15.rl), custom_call_target="tpu_custom_call" | custom-call | tf_op jit(solution)/shard_map/leave/pallas_call | solution.py:550

commit v5 on v4

--- a/solution.py
+++ b/solution.py
@@ -55,13 +55,21 @@
     return zs, ys, xs, [device_at(x, y, z, 1 - core)]
 
 
+FAR_FIRST = (4, 3, 5, 2, 6, 1, 7, 0)
+
+
+def plane_peers(x, y, z, core):
+    steps = [(dy, dz) for dz in FAR_FIRST for dy in FAR_FIRST if (dy, dz) != (0, 0)]
+    return [device_at(x, (y + dy) % NY, (z + dz) % NZ, core) for dy, dz in steps]
+
+
 def body(fields_hbm, w_hbm, bias_hbm, target_hbm, list_hbm, tail_hbm, weight_hbm,
          gf_out, gk_out, gb_out, rl_out,
          fields, w, bias, target, tiles_i, tail_i, weight_f, small, lwc,
          pad, shifted, turned, colbuf, rowbuf, colrec, rowrec, ds_ref, r1, r4, pt, es,
          gk, cbuf, crec, hx, hy, hz, sx, sy, sz, rx, ry, rz,
          hx2, sx2, rx2, sy2, ry2, sz2, rz2, ex, ey, ez, fy, fz, gb0, gbx, gby, gbz,
-         lsem, hsend, hrecv, gsend, grecv, asend, arecv):
+         plane_sem, lsem, hsend, hrecv, gsend, grecv, asend, arecv):
     lat, lon, x, y, z, core = position()
     loads = [
         pltpu.make_async_copy(src, dst, lsem.at[n])
@@ -137,6 +145,8 @@
     halo = halo_copies(0)
     for copy in halo:
         copy.start()
+    for peer in ys:
+        pl.semaphore_signal(plane_sem, inc=1, device_id=peer, device_id_type=MESH)
 
     for load in loads[1:4]:
         load.wait()
@@ -178,7 +188,7 @@
     lw_row = lat_weight((lax.broadcasted_iota(jnp.int32, (1, NPTS), 1) >> 4) & 7)
 
     slot = lax.broadcasted_iota(jnp.int32, (1024, 128), 0)
-    at_t, at_z, at_y = slot & 1, (slot >> 1) & 7, (slot >> 4) & 7
+    at_t, at_y, at_z = (slot >> 6) & 1, (slot >> 3) & 7, slot & 7
     at_x, at_c = (slot >> 7) & 3, slot >> 9
     tile = ((at_y >> 2) * 8 + at_z) * 64 + (at_x * 8 + (at_y & 3) * 2 + at_c) * 2 + at_t
     tile = tile.astype(F32)
@@ -213,8 +223,7 @@
         jnp.ones((8, C), F32), square, (((1,), (1,)), ((), ())),
         precision=lax.Precision.HIGHEST, preferred_element_type=F32,
     )[0:1, :] * (1.0 / C) * lw_row
-    r1[z, 0:1, :] = err_row[:, :128]
-    r1[z, 1:2, :] = err_row[:, 128:]
+    r1[8 * y + z] = err_row
 
     def exchange(ref, slot_id, peers, first):
         copies = [
@@ -229,22 +238,20 @@
         for k in taps:
             turned[k] = jnp.transpose(patch(k // 3, k % 3))
 
-    copies = exchange(r1, z, zs, 0)
+    pl.semaphore_wait(plane_sem, NY - 1)
+    copies = exchange(r1, 8 * y + z, plane_peers(x, y, z, core), 0)
     err_col = jnp.sum(square, axis=1, keepdims=True) * (1.0 / C) * lw_col
-    turn(range(4))
+    turn(range(9))
     for copy in copies:
         copy.wait()
-    for zz in range(NZ):
-        r4[core, x, y, 2 * zz : 2 * zz + 2, :] = r1[zz, 0:2, :]
-    copies = exchange(r4.at[core, x], y, ys, 7)
-    turn(range(4, 9))
-    for copy in copies:
-        copy.wait()
-    copies = exchange(r4.at[core], x, xs, 14)
-    passed = exchange(r4.at[core], x, cs, 17)
+    for n in range(NY * NZ):
+        r4[core, x, n : n + 1, :] = r1[n, :, :128]
+        r4[core, x, 64 + n : 65 + n, :] = r1[n, :, 128:]
+    copies = exchange(r4.at[core], x, xs, 63)
+    passed = exchange(r4.at[core], x, cs, 66)
     for n, k in enumerate((1, 3, 2)):
         copies[k - 1].wait()
-        passed += exchange(r4.at[core], (x + NX - k) % NX, cs, 18 + n)
+        passed += exchange(r4.at[core], (x + NX - k) % NX, cs, 67 + n)
     for copy in passed:
         copy.wait()
 
@@ -258,31 +265,35 @@
         part = jnp.dot(three, pt[:, 256 * blk : 256 * (blk + 1)], preferred_element_type=F32)
         es[:, 256 * blk : 256 * (blk + 1)] = part[:128] + part[128:256] + part[256:]
 
-    def fold(value):
-        total = value[:, 0:128]
-        for blk in range(1, 8):
-            total = total + value[:, 128 * blk : 128 * (blk + 1)]
-        total = jnp.sum(total, axis=0, keepdims=True)
-        total = jnp.broadcast_to(total, (8, 128))
+    def everywhere(total):
+        for shift in (4, 2, 1):
+            total = total + pltpu.roll(total, shift, 0)
         total = total + pltpu.roll(total, 64, 1)
         return total + pltpu.roll(total, 32, 1)
+
+    def over_points(terms):
+        totals = None
+        for blk in range(8):
+            block = es[:, 128 * blk : 128 * (blk + 1)].reshape(16, 8, 128)
+            sums = [jnp.sum(term, axis=0) for term in terms(block)]
+            totals = sums if totals is None else [a + b for a, b in zip(totals, sums)]
+        return [everywhere(total) for total in totals]
 
     points = float(NPTS // 2 * 32)
     count = jnp.broadcast_to(small[8:9, :], (8, 128))
     weight = jnp.broadcast_to(small[9:10, :], (8, 128))
 
-    def lanes(thresh):
-        return jnp.concatenate([thresh[0:1, :]] * 8, axis=1)
-
-    thresh = 2.0 * fold(es[...]) / points
+    thresh = 2.0 * over_points(lambda block: [block])[0] / points
 
     def iterate(_, thresh):
-        half = (es[...] - lanes(thresh)) * (0.5 / SMOOTH)
-        tangent = jnp.tanh(half)
-        above = 0.5 * (fold(tangent) + points)
-        spread = 0.25 * fold(1.0 - tangent * tangent)
+        def terms(block):
+            tangent = jnp.tanh((block - thresh) * (0.5 / SMOOTH))
+            return [tangent, 1.0 - tangent * tangent]
+
+        tangents, spreads = over_points(terms)
+        above = 0.5 * (tangents + points)
         return thresh + jnp.clip(
-            DAMPING * SMOOTH * (above - count) / (spread + 1.0), -STEP_LIMIT, STEP_LIMIT
+            DAMPING * SMOOTH * (above - count) / (0.25 * spreads + 1.0), -STEP_LIMIT, STEP_LIMIT
         )
 
     thresh = lax.fori_loop(0, ITERS, iterate, thresh)
@@ -394,9 +405,12 @@
     for t in range(2):
         gf_out[:, 16 * t : 16 * (t + 1), :] = total[t * 128 : (t + 1) * 128].reshape(ROWS, 16, C)
 
-    scaled = (es[...] - lanes(thresh)) * (1.0 / SMOOTH)
-    soft = jnp.maximum(scaled, 0.0) + jnp.log1p(jnp.exp(-jnp.abs(scaled)))
-    rl_out[...] = (thresh + SMOOTH * fold(soft) / count)[0:1, 0:NREG]
+    def softplus(block):
+        scaled = (block - thresh) * (1.0 / SMOOTH)
+        return [jnp.maximum(scaled, 0.0) + jnp.log1p(jnp.exp(-jnp.abs(scaled)))]
+
+    soft = over_points(softplus)[0]
+    rl_out[...] = (thresh + SMOOTH * soft / count)[0:1, 0:NREG]
 
     def gathered(own, received):
         for n in range(received.shape[0]):
@@ -523,7 +537,7 @@
             v((ROWS + 2, 48, C), F32), v((3, 2, ROWS + 2, 16, C), BF16), v((9, C, NPTS), BF16),
             v((2, 2, ROWS, C), F32), v((2, 2, COLS, C), BF16),
             v((2, 6, ROWS, C), F32), v((2, 2, COLS, C), BF16),
-            v((NPTS, C), F32), v((NZ, 8, 128), F32), v((2, NX, NY, 16, 128), F32),
+            v((NPTS, C), F32), v((NY * NZ, 1, 256), F32), v((2, NX, 128, 128), F32),
             v((1024, 1024), BF16), v((128, 1024), F32),
             v((2, 1152, C), F32), v((1152, C), BF16), v((1152, C), BF16),
             v((NX, 128, C), F32), v((NY, 48, C), F32), v((NZ, 32, C), F32),
@@ -535,7 +549,7 @@
             v((NZ, 16, C), BF16), v((NX, 8, C), F32), v((NY, 8, C), F32),
             v((NZ, 8, C), F32), v((NX, 8, C), F32),
             v((2, 1, C), F32), v((NX, 1, C), F32), v((NY, 1, C), F32), v((NZ, 1, C), F32),
-            dma((7,)), dma((2, 8)), dma((2, 8)), dma((21,)), dma((21,)), dma((110,)), dma((110,)),
+            pltpu.SemaphoreType.REGULAR, dma((7,)), dma((2, 8)), dma((2, 8)), dma((70,)), dma((70,)), dma((110,)), dma((110,)),
         ],
         compiler_params=pltpu.CompilerParams(
             collective_id=0, has_side_effects=True, vmem_limit_bytes=60 * 1024 * 1024

time: 81 us -> 79.1 us (0.977)
  Pallas kernels: 80.2 us -> 78.3 us
    pallas_call x1, Pallas kernels: 78.1 us -> 76.1 us  [on_device(): pl.pallas_call(body, out_shape=(jax.ShapeDtypeStruct((ROWS, COLS, C), BF1...]
where the time goes in v5:
time: 79.1 us; the launch traced here: 78.9 us
  Pallas kernels  78.3 us (99%)
    pallas_call x1, Pallas kernels, on_device(): pl.pallas_call(body, out_shape=(jax.ShapeDtypeStruct((ROWS, COLS, C), BF1...  76.1 us
    pallas_call x1, Pallas kernels, on_device(): pl.pallas_call(leave, out_shape=[jax.ShapeDtypeStruct(r.shape, r.dtype) f...  2.17 us

profile of v5, /device:TPU:1, one launch (start us, length us, event | category | flops | bytes accessed | tf_op | source)
XLA Modules:
  0.0 78.9 jit_solution(16394857026423381354)
XLA Ops:
  0.6 76.1 %layer.1 = (bf16[8,32,256]{2,1,0:T(8,128)(2,1)}, bf16[2,1152,256]{2,1,0:T(8,128)(2,1)}, f32[1,256]{1,0:T(1,128)}, f32[1,32]{1,0:T(1,128)}) custom-call(bf16[8,32,256]{2,1,0:T(8,128)(2,1)} %fields_hbm.1, bf16[2304,256]{1,0:T(8,128)(2,1)} %bitcast.8, f32[1,256]{1,0:T(1,128)} %bitcast.10, bf16[8,32,256]{2,1,0:T(8,128)(2,1)} %target_hbm.1, s32[8,128]{1,0:T(8,128)} %bitcast.9, ...), custom_call_target="tpu_custom_call" | custom-call | tf_op jit(solution)/shard_map/layer/pallas_call | solution.py:523
  76.7 2.2 %leave.1 = (bf16[8,32,256]{2,1,0:T(8,128)(2,1)}, bf16[2,1152,256]{2,1,0:T(8,128)(2,1)}, f32[1,256]{1,0:T(1,128)}, f32[1,32]{1,0:T(1,128)}) custom-call(bf16[8,32,256]{2,1,0:T(8,128)(2,1)} %get-tuple-element.12.gf, bf16[2,1152,256]{2,1,0:T(8,128)(2,1)} %get-tuple-element.13.gk, f32[1,256]{1,0:T(1,128)} %get-tuple-element.14.gb, f32[1,32]{1,0:T(1,128)} %get-tuple-element.15.rl), custom_call_target="tpu_custom_call" | custom-call | tf_op jit(solution)/shard_map/leave/pallas_call | solution.py:564
